TPU v7x, 32 devices: a whole 2x2x4 slice. The times are simulated.
32 devices in a mesh: dp: 4 (over y, x), hidden: 8 (over z, core).
Axes of the slice: x: 2, y: 2, z: 4, core: 2. Of those that a mesh axis runs over, the one named last changes fastest.
Arguments:
- activations: bfloat16 [6144, 1024], P('hidden', 'dp'), may hold values from -6 to 6
- cotangent: bfloat16 [6144, 1024], P('hidden', 'dp'), may hold values from -6 to 6
- in_blocks: bfloat16 [3, 1536, 24576], P(None, None, 'hidden'), may hold values from -0.09375 to 0.09375
- out_blocks: bfloat16 [3, 1536, 24576], P(None, None, 'hidden'), may hold values from -0.046875 to 0.046875
- in_left: bfloat16 [6144, 192], P('hidden'), may hold values from -0.078125 to 0.078125
- in_right: bfloat16 [192, 24576], P(None, 'hidden'), may hold values from -0.4375 to 0.4375
- out_left: bfloat16 [24576, 192], P('hidden'), may hold values from -0.0390625 to 0.0390625
- out_right: bfloat16 [6144, 192], P('hidden'), may hold values from -0.4375 to 0.4375
- factor_slots: int32 [2, 3], replicated, may hold values from 0 to 2, each once within a row
Outputs:
- output: bfloat16 [6144, 1024], P('hidden', 'dp')
- grad_input: bfloat16 [6144, 1024], P('hidden', 'dp')
- grad_in_blocks: float32 [3, 1536, 24576], P(None, None, 'hidden')
- grad_out_blocks: float32 [3, 1536, 24576], P(None, None, 'hidden')
- grad_in_left: float32 [6144, 192], P('hidden')
- grad_in_right: float32 [192, 24576], P(None, 'hidden')
- grad_out_left: float32 [24576, 192], P('hidden')
- grad_out_right: float32 [6144, 192], P('hidden')
Inputs may be any that keep to these rules, and one draw needn't show every extreme that they name: `factor_slots`: each row names every weight slice once.
All inputs are finite; a program needn't handle non-finite values.
Results may differ from a plain program's by a relative error of at most 0.006.
Values may be sent and summed in bfloat16 or wider, within the bound.
A program may use at most 576 MiB of HBM per device.

v0:
```python
import jax
import jax.numpy as jnp
from jax import lax
from jax.sharding import PartitionSpec as P


def partner_2(shard, axis, bit):
    return lax.ppermute(shard, axis, [(i, i ^ 1 << bit) for i in range(lax.axis_size(axis))])


def gelu_curve(values):
    return jax.nn.gelu(values, approximate=True)


def contract(former, latter):
    return lax.dot_general(
        former, latter, (((0,), (0,)), ((), ())), preferred_element_type=jnp.float32
    )


def outer_sum(former, latter):
    return lax.dot_general(
        former, latter, (((1,), (1,)), ((), ())), preferred_element_type=jnp.float32
    )


def matmul(former, latter):
    return jnp.dot(former, latter, preferred_element_type=jnp.float32)


def select_factor(weights, position):
    return lax.dynamic_index_in_dim(weights, position, 0, keepdims=False)


def swap_value(values, bit_number):
    return partner_2(values, "hidden", bit_number)


def swap_sum(values, bit_number):
    return partner_2(values, "hidden", bit_number)


def assemble(own_rows, lower_half):
    other_rows = partner_2(own_rows, "hidden", 0)
    first = jnp.where(lower_half, own_rows, other_rows)
    second = jnp.where(lower_half, other_rows, own_rows)
    return jnp.concatenate([first, second], axis=0)


def fold_halves(total, lower_half):
    rows_half = total.shape[0] // 2
    first = total[:rows_half]
    second = total[rows_half:]
    mine = jnp.where(lower_half, first, second)
    theirs = jnp.where(lower_half, second, first)
    return mine + partner_2(theirs, "hidden", 0)


def hidden_sum(partial_value):
    return lax.psum(partial_value, "hidden").astype(jnp.bfloat16)


def shards(
    activations,
    cotangent,
    in_blocks,
    out_blocks,
    in_left,
    in_right,
    out_left,
    out_right,
    factor_slots,
):
    levels = lax.axis_size("hidden").bit_length() - 2
    lower_half = lax.axis_index("hidden") % 2 == 0
    in_slots = [factor_slots[0, level] for level in range(levels + 1)]
    out_slots = [factor_slots[1, level] for level in range(levels + 1)]
    full_act = assemble(activations, lower_half)
    lowrank_in = hidden_sum(contract(in_left, activations))
    preact = contract(select_factor(in_blocks, in_slots[0]), full_act) + contract(
        in_right, lowrank_in
    )
    kept_partners = []
    for level in range(levels):
        partner = swap_value(full_act, level + 1)
        kept_partners.append(partner)
        preact = preact + contract(select_factor(in_blocks, in_slots[level + 1]), partner)
    act_float, gelu_back = jax.vjp(gelu_curve, preact)
    hidden_act = act_float.astype(jnp.bfloat16)
    lowrank_out = hidden_sum(contract(out_left, hidden_act))
    out_total = matmul(select_factor(out_blocks, out_slots[0]), hidden_act)
    for level in range(levels):
        out_total = out_total + swap_sum(
            matmul(select_factor(out_blocks, out_slots[level + 1]), hidden_act), level + 1
        )
    output = fold_halves(out_total, lower_half) + matmul(out_right, lowrank_out)
    full_cot = assemble(cotangent, lower_half)
    grad_low_out = hidden_sum(contract(out_right, cotangent))
    grad_act = matmul(out_left, grad_low_out) + contract(
        select_factor(out_blocks, out_slots[0]), full_cot
    )
    out_table = jnp.zeros(out_blocks.shape, jnp.float32)
    out_table = lax.dynamic_update_index_in_dim(
        out_table, outer_sum(full_cot, hidden_act), out_slots[0], 0
    )
    for level in range(levels):
        partner_cot = swap_value(full_cot, level + 1)
        grad_act = grad_act + contract(select_factor(out_blocks, out_slots[level + 1]), partner_cot)
        out_table = lax.dynamic_update_index_in_dim(
            out_table, outer_sum(partner_cot, hidden_act), out_slots[level + 1], 0
        )
    grad_pre = gelu_back(grad_act)[0].astype(jnp.bfloat16)
    grad_low_in = hidden_sum(matmul(in_right, grad_pre))
    in_total = matmul(select_factor(in_blocks, in_slots[0]), grad_pre)
    in_table = jnp.zeros(in_blocks.shape, jnp.float32)
    in_table = lax.dynamic_update_index_in_dim(
        in_table, outer_sum(full_act, grad_pre), in_slots[0], 0
    )
    for level in range(levels):
        in_total = in_total + swap_sum(
            matmul(select_factor(in_blocks, in_slots[level + 1]), grad_pre), level + 1
        )
        partner = swap_value(full_act, level + 1)
        in_table = lax.dynamic_update_index_in_dim(
            in_table, outer_sum(partner, grad_pre), in_slots[level + 1], 0
        )
    grad_input = fold_halves(in_total, lower_half) + matmul(in_left, grad_low_in)
    totals = lax.psum(
        (
            in_table,
            out_table,
            outer_sum(activations, grad_low_in),
            outer_sum(lowrank_in, grad_pre),
            outer_sum(hidden_act, grad_low_out),
            outer_sum(cotangent, lowrank_out),
        ),
        "dp",
    )
    norm_scale = (lax.axis_size("dp") * activations.shape[1]) ** (-0.5)
    return (
        output.astype(jnp.bfloat16),
        grad_input.astype(jnp.bfloat16),
        totals[0] * norm_scale,
        totals[1] * norm_scale,
        totals[2] * norm_scale,
        totals[3] * norm_scale,
        totals[4] * norm_scale,
        totals[5] * norm_scale,
    )


def solution(mesh):
    return jax.shard_map(
        shards,
        mesh=mesh,
        in_specs=(
            P("hidden", "dp"),
            P("hidden", "dp"),
            P(None, None, "hidden"),
            P(None, None, "hidden"),
            P("hidden", None),
            P(None, "hidden"),
            P("hidden", None),
            P("hidden", None),
            P(),
        ),
        out_specs=(
            P("hidden", "dp"),
            P("hidden", "dp"),
            P(None, None, "hidden"),
            P(None, None, "hidden"),
            P("hidden", None),
            P(None, "hidden"),
            P("hidden", None),
            P("hidden", None),
        ),
        check_vma=False,
    )
```

profile of v0, /device:TPU:0, one launch (start us, length us, event | category | flops | bytes accessed | tf_op | source)
XLA Modules:
  0.0 2366.0 jit_solution(12896018962152926021)
XLA Ops:
  7.8 1.3 fusion.98
  9.2 1.3 fusion.99
  10.5 35.3 %all-reduce.8 = (bf16[192,256]{1,0:T(8,128)(2,1)S(1)}, bf16[192,256]{1,0:T(8,128)(2,1)S(1)}) all-reduce(f32[192,256]{1,0:T(8,128)S(1)} %fusion.98, f32[192,256]{1,0:T(8,128)S(1)} %fusion.99), channel_id=1, replica_groups=mesh['dp'=4,'hidden'=8] {'hidden'}, use_global_device_ids=true, to_apply=%region_0.1 | all-reduce | flops 98304 | bytes 589824 | tf_op jit(solution)/shard_map/psum | solution.py:60
  45.8 1.5 fusion.97
  59.0 2.0 convolution_bitcast_fusion.1
  62.5 1.8 collective-permute-start.7
  64.4 2.9 collective-permute-start.8
  67.3 29.3 %collective-permute-done.2 = bf16[1536,256]{1,0:T(8,128)(2,1)S(1)} collective-permute-done((bf16[1536,256]{1,0:T(8,128)(2,1)S(1)}, bf16[1536,256]{1,0:T(8,128)(2,1)S(1)}, u32[]{:S(2)}, u32[]{:S(2)}) %collective-permute-start.2) | collective-permute-done | bytes 786464 | tf_op jit(solution)/shard_map/ppermute | solution.py:8
  96.6 8.4 fusion.10
  105.0 9.6 collective-permute-done.1
  114.6 8.4 fusion.14
  123.0 9.6 multiply_convert_fusion
  132.7 1.2 convolution_bitcast_fusion.7
  133.8 2.4 fusion.100
  136.2 8.4 fusion
  144.7 8.4 fusion.4
  153.1 10.5 fusion.60
  163.6 1.2 convolution_bitcast_fusion.6
  164.8 2.1 fusion.101
  166.9 31.2 %all-reduce.9 = (bf16[192,256]{1,0:T(8,128)(2,1)S(1)}, bf16[192,256]{1,0:T(8,128)(2,1)S(1)}) all-reduce(f32[192,256]{1,0:T(8,128)S(1)} %copy-done.27, f32[192,256]{1,0:T(8,128)S(1)} %copy-done.28), channel_id=1, replica_groups=mesh['dp'=4,'hidden'=8] {'hidden'}, use_global_device_ids=true, to_apply=%region_1.2 | all-reduce | flops 98304 | bytes 589824 | tf_op jit(solution)/shard_map/psum | solution.py:60
  198.1 1.1 convolution_bitcast_fusion.4
  199.2 1.1 convolution_bitcast_fusion.5
  200.4 18.5 broadcast.27.clone
  218.8 8.3 bitcast_dynamic-update-slice_fusion.5
  227.1 18.5 broadcast.27.clone.1
  245.6 8.3 bitcast_dynamic-update-slice_fusion.2
  253.9 8.3 bitcast_dynamic-update-slice_fusion.4
  262.2 8.3 bitcast_dynamic-update-slice_fusion.3
  270.5 8.3 bitcast_dynamic-update-slice_fusion.1
  278.8 8.3 bitcast_dynamic-update-slice_fusion
  287.1 5.2 fusion.6
  292.4 5.3 fusion.2
  297.7 1.3 collective-permute-start.4
  299.0 5.8 fusion.8
  304.8 5.5 fusion.12
  310.4 1.0 collective-permute-start.9
  311.4 2.8 collective-permute-start.10
  314.2 42.4 %collective-permute-done.3 = f32[1536,256]{1,0:T(8,128)S(1)} collective-permute-done((f32[1536,256]{1,0:T(8,128)S(1)}, f32[1536,256]{1,0:T(8,128)S(1)}, u32[]{:S(2)}, u32[]{:S(2)}) %collective-permute-start.3) | collective-permute-done | bytes 1572896 | tf_op jit(solution)/shard_map/ppermute | solution.py:8
  356.6 13.1 collective-permute-done.4
  369.8 5.2 fusion.70
  375.2 44.0 %collective-permute-done.9 = f32[1536,256]{1,0:T(8,128)S(1)} collective-permute-done((f32[1536,256]{1,0:T(8,128)S(1)}, f32[1536,256]{1,0:T(8,128)S(1)}, u32[]{:S(2)}, u32[]{:S(2)}) %collective-permute-start.9) | collective-permute-done | bytes 1572896 | tf_op jit(solution)/shard_map/ppermute | solution.py:8
  419.2 16.0 collective-permute-done.10
  435.2 5.7 fusion.67
  444.4 1833.9 %all-reduce.7.cloned.1.call-done = (f32[3,1536,3072]{2,1,0:T(8,128)}, f32[3,1536,3072]{2,1,0:T(8,128)}, f32[768,192]{0,1:T(8,128)}, f32[192,3072]{1,0:T(8,128)}, f32[3072,192]{0,1:T(8,128)}, /*index=5*/f32[768,192]{0,1:T(8,128)}) async-done(((f32[3,1536,3072]{2,1,0:T(8,128)}, f32[3,1536,3072]{2,1,0:T(8,128)}, f32[768,192]{0,1:T(8,128)}, f32[192,3072]{1,0:T(8,128)}, f32[3072,192]{0,1:T(8,128)}, ...) | async-done | bytes 119144464 | tf_op jit(solution)/shard_map/psum | solution.py:128
  2278.2 3.5 broadcast_multiply_fusion.3
  2281.7 1.6 broadcast_multiply_fusion.2
  2283.3 74.6 %broadcast_multiply_fusion = (f32[3,1536,3072]{2,1,0:T(8,128)}, f32[3,1536,3072]{2,1,0:T(8,128)}) fusion(f32[3,1536,3072]{2,1,0:T(8,128)} %get-tuple-element.13, f32[3,1536,3072]{2,1,0:T(8,128)} %get-tuple-element.12), kind=kLoop, calls=%fused_computation | loop fusion | flops 28311552 | bytes 226492416 | tf_op jit(solution)/shard_map/mul | solution.py:144
  2357.9 1.1 broadcast_multiply_fusion.4
  (100 shorter events, 5.8 us)
Async XLA Ops:
  7.2 54.1 %copy-start = (bf16[3072,192]{0,1:T(8,128)(2,1)S(1)}, bf16[3072,192]{0,1:T(8,128)(2,1)}, u32[]{:S(2)}) copy-start(bf16[3072,192]{0,1:T(8,128)(2,1)} %param.15) | copy-start | bytes 3538948
  7.2 53.8 %copy-start.7 = (bf16[768,256]{1,0:T(8,128)(2,1)S(1)}, bf16[768,256]{1,0:T(8,128)(2,1)}, u32[]{:S(2)}) copy-start(bf16[768,256]{1,0:T(8,128)(2,1)} %param.9) | copy-start | bytes 1179652
  7.2 2271.0 %all-reduce.7.cloned.1.call-start = ((), (), s32[]{:S(2)}) async-start(), calls=%async_computation | async-start | bytes 238288896 | tf_op jit(solution)/shard_map/psum | solution.py:128
  7.2 53.8 %collective-permute-start = (bf16[768,256]{1,0:T(8,128)(2,1)}, bf16[768,256]{1,0:T(8,128)(2,1)S(1)}, u32[]{:S(2)}, u32[]{:S(2)}) collective-permute-start(bf16[768,256]{1,0:T(8,128)(2,1)} %param.9), channel_id=1, source_target_pairs={{0,1},{1,0},{2,3},{3,2},{4,5},{5,4},{6,7},{7,6},{8,9},{9,8},{10,11... | collective-permute-start | bytes 1179656 | tf_op jit(solution)/shard_map/ppermute | solution.py:8
  7.8 54.5 %collective-permute-start.6 = (bf16[768,256]{1,0:T(8,128)(2,1)}, bf16[768,256]{1,0:T(8,128)(2,1)S(1)}, u32[]{:S(2)}, u32[]{:S(2)}) collective-permute-start(bf16[768,256]{1,0:T(8,128)(2,1)} %param.10), channel_id=1, source_target_pairs={{0,1},{1,0},{2,3},{3,2},{4,5},{5,4},{6,7},{7,6},{8,9},{9,8},{10,11... | collective-permute-start | bytes 1179656 | tf_op jit(solution)/shard_map/ppermute | solution.py:8
  45.8 15.4 copy-start.33
  45.8 15.5 copy-start.35
  61.1 61.9 %copy-start.8 = (bf16[768,256]{1,0:T(8,128)(2,1)}, bf16[768,256]{1,0:T(8,128)(2,1)S(1)}, u32[]{:S(2)}) copy-start(bf16[768,256]{1,0:T(8,128)(2,1)S(1)} %get-tuple-element.20) | copy-start | bytes 1179652
  61.1 61.9 %copy-start.10 = (bf16[768,256]{1,0:T(8,128)(2,1)}, bf16[768,256]{1,0:T(8,128)(2,1)S(1)}, u32[]{:S(2)}) copy-start(bf16[768,256]{1,0:T(8,128)(2,1)S(1)} %get-tuple-element.21) | copy-start | bytes 1179652
  61.1 1.3 copy-start.6
  61.2 35.4 %collective-permute-start.2 = (bf16[1536,256]{1,0:T(8,128)(2,1)S(1)}, bf16[1536,256]{1,0:T(8,128)(2,1)S(1)}, u32[]{:S(2)}, u32[]{:S(2)}) collective-permute-start(bf16[1536,256]{1,0:T(8,128)(2,1)S(1)} %pad_maximum_fusion), channel_id=1, source_target_pairs={{0,4},{1,5},{2,6},{3,7},{4,0},{5,1},{6,2},{7,3},{8,12},{9,13},{10,... | collective-permute-start | bytes 2359304 | tf_op jit(solution)/shard_map/ppermute | solution.py:8
  62.1 52.5 %collective-permute-start.1 = (bf16[1536,256]{1,0:T(8,128)(2,1)S(1)}, bf16[1536,256]{1,0:T(8,128)(2,1)S(1)}, u32[]{:S(2)}, u32[]{:S(2)}) collective-permute-start(bf16[1536,256]{1,0:T(8,128)(2,1)S(1)} %pad_maximum_fusion), channel_id=1, source_target_pairs={{0,2},{1,3},{2,0},{3,1},{4,6},{5,7},{6,4},{7,5},{8,10},{9,11},{10,... | collective-permute-start | bytes 2359304 | tf_op jit(solution)/shard_map/ppermute | solution.py:8
  62.5 90.6 %copy-start.12 = (bf16[768,256]{1,0:T(8,128)(2,1)}, bf16[768,256]{1,0:T(8,128)(2,1)S(1)}, u32[]{:S(2)}) copy-start(bf16[768,256]{1,0:T(8,128)(2,1)S(1)} %get-tuple-element.18) | copy-start | bytes 1179652
  62.5 90.6 %copy-start.14 = (bf16[768,256]{1,0:T(8,128)(2,1)}, bf16[768,256]{1,0:T(8,128)(2,1)S(1)}, u32[]{:S(2)}) copy-start(bf16[768,256]{1,0:T(8,128)(2,1)S(1)} %get-tuple-element.19) | copy-start | bytes 1179652
  62.5 82.1 %collective-permute-start.7 = (bf16[1536,256]{1,0:T(8,128)(2,1)S(1)}, bf16[1536,256]{1,0:T(8,128)(2,1)S(1)}, u32[]{:S(2)}, u32[]{:S(2)}) collective-permute-start(bf16[1536,256]{1,0:T(8,128)(2,1)S(1)} %pad_maximum_fusion.1), channel_id=1, source_target_pairs={{0,2},{1,3},{2,0},{3,1},{4,6},{5,7},{6,4},{7,5},{8,10},{9,11},{10,... | collective-permute-start | bytes 2359304 | tf_op jit(solution)/shard_map/ppermute | solution.py:8
  64.4 71.9 %collective-permute-start.8 = (bf16[1536,256]{1,0:T(8,128)(2,1)S(1)}, bf16[1536,256]{1,0:T(8,128)(2,1)S(1)}, u32[]{:S(2)}, u32[]{:S(2)}) collective-permute-start(bf16[1536,256]{1,0:T(8,128)(2,1)S(1)} %pad_maximum_fusion.1), channel_id=1, source_target_pairs={{0,4},{1,5},{2,6},{3,7},{4,0},{5,1},{6,2},{7,3},{8,12},{9,13},{10,... | collective-permute-start | bytes 2359304 | tf_op jit(solution)/shard_map/ppermute | solution.py:8
  96.6 8.4 copy-start.19
  114.6 8.4 copy-start.21
  123.0 10.8 copy-start.36
  136.2 8.4 copy-start.25
  144.7 8.4 copy-start.23
  153.1 10.5 copy-start.5
  153.1 11.7 copy-start.34
  163.6 1.2 copy-start.2
  164.8 2.1 copy-start.27
  164.8 2.1 copy-start.28
  200.4 18.5 copy-start.3
  200.4 18.5 copy-start.9
  200.4 18.5 copy-start.11
  227.1 18.5 copy-start.13
  227.1 18.5 copy-start.15
  245.6 8.3 copy-start.22
  253.9 8.3 copy-start.20
  262.2 8.3 copy-start.24
  270.5 8.3 copy-start.26
  292.3 6.7 copy-start.4
  292.3 64.3 %collective-permute-start.3 = (f32[1536,256]{1,0:T(8,128)S(1)}, f32[1536,256]{1,0:T(8,128)S(1)}, u32[]{:S(2)}, u32[]{:S(2)}) collective-permute-start(f32[1536,256]{1,0:T(8,128)S(1)} %fusion.6), channel_id=1, source_target_pairs={{0,2},{1,3},{2,0},{3,1},{4,6},{5,7},{6,4},{7,5},{8,10},{9,11},{10,... | collective-permute-start | bytes 4718600 | tf_op jit(solution)/shard_map/ppermute | solution.py:8
  297.7 72.1 %collective-permute-start.4 = (f32[1536,256]{1,0:T(8,128)S(1)}, f32[1536,256]{1,0:T(8,128)S(1)}, u32[]{:S(2)}, u32[]{:S(2)}) collective-permute-start(f32[1536,256]{1,0:T(8,128)S(1)} %fusion.2), channel_id=1, source_target_pairs={{0,4},{1,5},{2,6},{3,7},{4,0},{5,1},{6,2},{7,3},{8,12},{9,13},{10,... | collective-permute-start | bytes 4718600 | tf_op jit(solution)/shard_map/ppermute | solution.py:8
  310.4 108.8 %collective-permute-start.9 = (f32[1536,256]{1,0:T(8,128)S(1)}, f32[1536,256]{1,0:T(8,128)S(1)}, u32[]{:S(2)}, u32[]{:S(2)}) collective-permute-start(f32[1536,256]{1,0:T(8,128)S(1)} %fusion.12), channel_id=1, source_target_pairs={{0,2},{1,3},{2,0},{3,1},{4,6},{5,7},{6,4},{7,5},{8,10},{9,11},{10,... | collective-permute-start | bytes 4718600 | tf_op jit(solution)/shard_map/ppermute | solution.py:8
  311.4 123.8 %collective-permute-start.10 = (f32[1536,256]{1,0:T(8,128)S(1)}, f32[1536,256]{1,0:T(8,128)S(1)}, u32[]{:S(2)}, u32[]{:S(2)}) collective-permute-start(f32[1536,256]{1,0:T(8,128)S(1)} %fusion.8), channel_id=1, source_target_pairs={{0,4},{1,5},{2,6},{3,7},{4,0},{5,1},{6,2},{7,3},{8,12},{9,13},{10,... | collective-permute-start | bytes 4718600 | tf_op jit(solution)/shard_map/ppermute | solution.py:8
  375.1 66.0 %copy-start.17 = (bf16[768,192]{0,1:T(8,128)(2,1)S(1)}, bf16[768,192]{0,1:T(8,128)(2,1)}, u32[]{:S(2)}) copy-start(bf16[768,192]{0,1:T(8,128)(2,1)} %param.13) | copy-start | bytes 884740
  375.1 66.0 %copy-start.32 = (bf16[192,256]{1,0:T(8,128)(2,1)S(1)}, bf16[192,256]{1,0:T(8,128)(2,1)}, u32[]{:S(2)}) copy-start(bf16[192,256]{1,0:T(8,128)(2,1)} %copy-done.31) | copy-start | bytes 294916
  375.1 67.1 %collective-permute-start.5 = (f32[768,256]{1,0:T(8,128)S(1)}, f32[768,256]{1,0:T(8,128)S(1)}, u32[]{:S(2)}, u32[]{:S(2)}) collective-permute-start(f32[768,256]{1,0:T(8,128)S(1)} %slice_select_fusion.1), channel_id=1, source_target_pairs={{0,1},{1,0},{2,3},{3,2},{4,5},{5,4},{6,7},{7,6},{8,9},{9,8},{10,11... | collective-permute-start | bytes 2359304 | tf_op jit(solution)/shard_map/ppermute | solution.py:8
  441.0 2.4 collective-permute-start.11
  2278.2 3.5 copy-start.16
  2283.3 74.6 %copy-start.29 = (f32[768,192]{0,1:T(8,128)S(1)}, f32[768,192]{0,1:T(8,128)}, u32[]{:S(2)}) copy-start(f32[768,192]{0,1:T(8,128)} %get-tuple-element.14) | copy-start | bytes 1769476
  2283.3 74.6 %copy-start.30 = (f32[768,192]{0,1:T(8,128)S(1)}, f32[768,192]{0,1:T(8,128)}, u32[]{:S(2)}) copy-start(f32[768,192]{0,1:T(8,128)} %get-tuple-element.17) | copy-start | bytes 1769476
  2283.3 75.7 %copy-start.1 = (bf16[3072,192]{0,1:T(8,128)(2,1)S(1)}, bf16[3072,192]{0,1:T(8,128)(2,1)}, u32[]{:S(2)}) copy-start(bf16[3072,192]{0,1:T(8,128)(2,1)} %param.15) | copy-start | bytes 3538948
  (2 other events, 2.1 us)
Sparse Core Ops, SparseCore 0:
  287.2 1991.0 all-reduce.6
where the time goes:
time: 2380 us; the launch traced here: 2370 us
  waiting for transfers between devices  1990 us (84%)
  matrix products  151 us (6%)
  other arithmetic  83 us (3%)
  blocking collectives  66.5 us (3%)
  local copies, waits for them, and re-layouts  39.2 us (2%)
  between operations  26.4 us (1%)
    psum x1, waiting for transfers between devices, shards(): lax.psum((in_table, out_table, outer_sum(activations, grad_low_in), outer...  1830 us
    ppermute x12, waiting for transfers between devices, partner_2(): lax.ppermute(shard, axis, [(i, i ^ 1 << bit) for i in range(lax.axis_size...  155 us
    mul x1, other arithmetic, shards(): totals[1] * norm_scale  74.6 us
    psum x2, blocking collectives, hidden_sum(): return lax.psum(partial_value, 'hidden').astype(jnp.bfloat16)  66.5 us
    dot_general x10, matrix products, contract(): lax.dot_general(former, latter, (((0,), (0,)), ((), ())), preferred_eleme...  59.6 us
    dot_general x10, matrix products, outer_sum(): lax.dot_general(former, latter, (((1,), (1,)), ((), ())), preferred_eleme...  56.4 us
  transfers between devices with their start and end apart: 13, of which 8 were waited for; matrix products, arithmetic and copies ran while one was open for 3% of the time, Pallas kernels for 0%

commit v1 on v0

v1 whole, which is shorter than its diff:
```python
import jax
import jax.numpy as jnp
from jax import lax
from jax.sharding import PartitionSpec as P


def dots(former, latter, left, right):
    return lax.dot_general(
        former, latter, (((left,), (right,)), ((), ())), preferred_element_type=jnp.float32
    )


def swap(values, bit):
    return lax.ppermute(
        values, "hidden", [(i, i ^ 1 << bit) for i in range(lax.axis_size("hidden"))]
    )


def by_slot(pieces, slots):
    rows = []
    for slot in range(len(pieces)):
        chosen = pieces[-1]
        for level in range(len(pieces) - 1):
            chosen = jnp.where(slots[level] == slot, pieces[level], chosen)
        rows.append(chosen)
    return jnp.stack(rows)


def pick(values, slot, axis=0):
    return lax.dynamic_index_in_dim(values, slot, axis, keepdims=False)


def both_halves(mine, other, is_first, axis):
    first = jnp.where(is_first, mine, other)
    second = jnp.where(is_first, other, mine)
    return jnp.stack([first, second], axis=axis)


def near_parts(own, slots, levels):
    return by_slot([own] + [swap(own, level + 1) for level in range(levels)], slots)


def gather(values):
    return lax.all_gather(values, "dp", axis=0, tiled=False)


def all_tokens(gathered, is_first):
    groups, factors, rows, tokens = gathered.shape
    full = both_halves(gathered, swap(gathered, 0), is_first, 2)
    return full.transpose(1, 2, 3, 0, 4).reshape(factors * 2 * rows, groups * tokens)


def flat_tokens(gathered):
    groups, rows, tokens = gathered.shape
    return gathered.transpose(1, 0, 2).reshape(rows, groups * tokens)


def reduce_blocks(part, slots, half, levels):
    theirs = pick(part, 1 - half, 1).astype(jnp.bfloat16)
    mine = pick(part, half, 1)
    total = mine + swap(theirs, 0).astype(jnp.float32)
    result = pick(total, slots[0])
    for level in range(levels):
        sent = pick(total, slots[level + 1]).astype(jnp.bfloat16)
        result = result + swap(sent, level + 1).astype(jnp.float32)
    return result


def shards(
    activations,
    cotangent,
    in_blocks,
    out_blocks,
    in_left,
    in_right,
    out_left,
    out_right,
    factor_slots,
):
    levels = lax.axis_size("hidden").bit_length() - 2
    factors = levels + 1
    half = lax.axis_index("hidden") % 2
    is_first = half == 0
    in_slots = [factor_slots[0, level] for level in range(factors)]
    out_slots = [factor_slots[1, level] for level in range(factors)]
    rows, tokens = activations.shape
    rank = in_left.shape[1]
    units = in_blocks.shape[2]
    scale = (lax.axis_size("dp") * tokens) ** (-0.5)
    in_flat = in_blocks.reshape(factors * 2 * rows, units)
    out_flat = out_blocks.reshape(factors * 2 * rows, units)

    act_near = near_parts(activations, in_slots, levels)
    cot_near = near_parts(cotangent, out_slots, levels)
    act_full = both_halves(act_near, swap(act_near, 0), is_first, 1)
    act_full = act_full.reshape(factors * 2 * rows, tokens)
    cot_full = both_halves(cot_near, swap(cot_near, 0), is_first, 1)
    cot_full = cot_full.reshape(factors * 2 * rows, tokens)

    low_first = lax.psum(
        jnp.concatenate(
            [dots(in_left, activations, 0, 0), dots(out_right, cotangent, 0, 0)], axis=0
        ),
        "hidden",
    ).astype(jnp.bfloat16)
    lowrank_in, grad_low_out = low_first[:rank], low_first[rank:]

    preact = dots(act_full, in_flat, 0, 0) + dots(lowrank_in, in_right, 0, 0)
    act_float, gelu_back = jax.vjp(lambda v: jax.nn.gelu(v, approximate=True), preact)
    hidden_act = act_float.astype(jnp.bfloat16)
    hidden_all = gather(hidden_act)
    grad_act = dots(cot_full, out_flat, 0, 0) + dots(grad_low_out, out_left, 0, 1)
    grad_pre = gelu_back(grad_act)[0].astype(jnp.bfloat16)
    pre_all = gather(grad_pre)
    cot_near_all = gather(cot_near)
    act_near_all = gather(act_near)
    first_all = flat_tokens(gather(low_first))

    low_last = lax.psum(
        jnp.concatenate(
            [dots(out_left, hidden_act, 0, 1), dots(in_right, grad_pre, 1, 1)], axis=0
        ),
        "hidden",
    ).astype(jnp.bfloat16)
    lowrank_out, grad_low_in = low_last[:rank], low_last[rank:]
    last_all = flat_tokens(gather(low_last))

    out_part = dots(out_flat, hidden_act, 1, 1).reshape(factors, 2, rows, tokens)
    in_part = dots(in_flat, grad_pre, 1, 1).reshape(factors, 2, rows, tokens)
    output = reduce_blocks(out_part, out_slots, half, levels) + dots(out_right, lowrank_out, 1, 0)
    grad_input = reduce_blocks(in_part, in_slots, half, levels) + dots(in_left, grad_low_in, 1, 0)

    hidden_all = hidden_all.reshape(-1, units)
    pre_all = pre_all.reshape(-1, units)
    cot_all = all_tokens(cot_near_all, is_first)
    act_all = all_tokens(act_near_all, is_first)
    grad_out_blocks = (dots(cot_all, hidden_all, 1, 0) * scale).reshape(out_blocks.shape)
    grad_in_blocks = (dots(act_all, pre_all, 1, 0) * scale).reshape(in_blocks.shape)
    own_act = flat_tokens(pick(act_near_all, in_slots[0], 1))
    own_cot = flat_tokens(pick(cot_near_all, out_slots[0], 1))
    return (
        output.astype(jnp.bfloat16),
        grad_input.astype(jnp.bfloat16),
        grad_in_blocks,
        grad_out_blocks,
        dots(own_act, last_all[rank:], 1, 1) * scale,
        dots(first_all[:rank], pre_all, 1, 0) * scale,
        dots(hidden_all, first_all[rank:], 0, 1) * scale,
        dots(own_cot, last_all[:rank], 1, 1) * scale,
    )


def solution(mesh):
    return jax.shard_map(
        shards,
        mesh=mesh,
        in_specs=(
            P("hidden", "dp"),
            P("hidden", "dp"),
            P(None, None, "hidden"),
            P(None, None, "hidden"),
            P("hidden", None),
            P(None, "hidden"),
            P("hidden", None),
            P("hidden", None),
            P(),
        ),
        out_specs=(
            P("hidden", "dp"),
            P("hidden", "dp"),
            P(None, None, "hidden"),
            P(None, None, "hidden"),
            P("hidden", None),
            P(None, "hidden"),
            P("hidden", None),
            P("hidden", None),
        ),
        check_vma=False,
    )
```

time: 2380 us -> 475 us (0.20)
  waiting for transfers between devices: 1990 us -> 29.2 us
  local copies, waits for them, and re-layouts: 39.2 us -> 76.5 us
  blocking collectives: 66.5 us -> 98.7 us
  other arithmetic: 83 us -> 51.7 us
    psum x1 -> x0, waiting for transfers between devices: 1830 us -> none  [shards(): lax.psum((in_table, out_table, outer_sum(activations, grad_low_in), outer...]
    ppermute x12 -> x14, waiting for transfers between devices: 155 us -> 29.2 us  [swap(): lax.ppermute(values, 'hidden', [(i, i ^ 1 << bit) for i in range(lax.axis...]
    mul x4 -> x0, other arithmetic: 80.7 us -> none  [the longest x1 74.6 us: shards(): totals[1] * norm_scale]
    another operation x0 -> x11, other arithmetic: none -> 37.8 us  [the longest x7 33.1 us: both_halves(): return jnp.stack([first, second], axis=axis)]
    another operation x2 -> x1, local copies, waits for them, and re-layouts: 36.9 us -> 0.15 us  [both_halves(): return jnp.stack([first, second], axis=axis)]
    all_gather x0 -> x2, blocking collectives: none -> 33.1 us  [gather(): return lax.all_gather(values, 'dp', axis=0, tiled=False)]
    unnamed x74 -> x62, local copies, waits for them, and re-layouts: 0.74 us -> 28.8 us
    dot_general x30 -> x18, matrix products: 151 us -> 162 us  [dots(): lax.dot_general(former, latter, (((left,), (right,)), ((), ())), preferre...]
  transfers between devices with their start and end apart: 13 -> 18, of which waited for: 8 -> 5; matrix products, arithmetic and copies ran while one was open for 3% -> 38% of each run, Pallas kernels for 0% -> 0%
where the time goes in v1:
time: 475 us; the launch traced here: 466 us
  matrix products  162 us (34%)
  blocking collectives  98.7 us (21%)
  local copies, waits for them, and re-layouts  76.5 us (16%)
  other arithmetic  51.7 us (11%)
  between operations  34.4 us (7%)
  waiting for transfers between devices  29.2 us (6%)
  starting transfers between devices  13.3 us (3%)
    dot_general x18, matrix products, dots(): lax.dot_general(former, latter, (((left,), (right,)), ((), ())), preferre...  162 us
    psum x1, blocking collectives, shards(): lax.psum(jnp.concatenate([dots(in_left, activations, 0, 0), dots(out_righ...  34.4 us
    all_gather x2, blocking collectives, gather(): return lax.all_gather(values, 'dp', axis=0, tiled=False)  33.1 us
    another operation x7, other arithmetic, both_halves(): return jnp.stack([first, second], axis=axis)  33.1 us
    psum x1, blocking collectives, shards(): lax.psum(jnp.concatenate([dots(out_left, hidden_act, 0, 1), dots(in_right...  31.2 us
    ppermute x14, waiting for transfers between devices, swap(): lax.ppermute(values, 'hidden', [(i, i ^ 1 << bit) for i in range(lax.axis...  29.2 us
    unnamed x62, local copies, waits for them, and re-layouts  28.8 us
    all_gather x2, local copies, waits for them, and re-layouts, gather(): return lax.all_gather(values, 'dp', axis=0, tiled=False)  16.5 us
  transfers between devices with their start and end apart: 18, of which 5 were waited for; matrix products, arithmetic and copies ran while one was open for 38% of the time, Pallas kernels for 0%

profile of v1, /device:TPU:0, one launch (start us, length us, event | category | flops | bytes accessed | tf_op | source)
XLA Modules:
  0.0 466.4 jit_solution(13603983681881465532)
XLA Ops:
  7.2 3.1 collective-permute-start.6
  10.3 2.6 collective-permute-start.7
  12.9 1.6 fusion.49
  18.4 9.6 %collective-permute-done.6 = bf16[768,256]{1,0:T(8,128)(2,1)S(1)} collective-permute-done((bf16[768,256]{1,0:T(8,128)(2,1)}, bf16[768,256]{1,0:T(8,128)(2,1)S(1)}, u32[]{:S(2)}, u32[]{:S(2)}) %collective-permute-start.6) | collective-permute-done | bytes 393248 | tf_op jit(solution)/shard_map/ppermute | solution.py:14
  28.0 2.5 collective-permute-done.7
  33.2 2.7 collective-permute-start
  39.9 10.1 %collective-permute-done.1 = bf16[768,256]{1,0:T(8,128)(2,1)S(1)} collective-permute-done((bf16[768,256]{1,0:T(8,128)(2,1)S(1)}, bf16[768,256]{1,0:T(8,128)(2,1)S(1)}, u32[]{:S(2)}, u32[]{:S(2)}) %collective-permute-start.1) | collective-permute-done | bytes 393248 | tf_op jit(solution)/shard_map/ppermute | solution.py:14
  56.8 34.4 %all-reduce.2 = bf16[384,256]{1,0:T(8,128)(2,1)} all-reduce(f32[384,256]{1,0:T(8,128)} %pad_maximum_fusion.5), channel_id=1, replica_groups=mesh['dp'=4,'hidden'=8] {'hidden'}, use_global_device_ids=true, to_apply=%region_0.1 | all-reduce | flops 98304 | bytes 589824 | tf_op jit(solution)/shard_map/psum | solution.py:100
  91.3 1.5 select_bitcast_fusion.7
  93.0 13.6 %fusion.50 = f32[256,3072]{1,0:T(8,128)S(1)} fusion(bf16[4608,256]{1,0:T(8,128)(2,1)S(1)} %bitcast.195, bf16[4608,3072]{1,0:T(8,128)(2,1)} %bitcast.181), kind=kOutput, calls=%fused_computation.93 | convolution fusion | flops 7247757312 | bytes 33816576 | tf_op jit(solution)/shard_map/dot_general | solution.py:8
  106.6 3.6 multiply_convert_fusion
  110.3 2.8 collective-permute-done.8
  113.8 13.9 %fusion.53 = f32[256,3072]{1,0:T(8,128)S(1)} fusion(bf16[4608,256]{1,0:T(8,128)(2,1)S(1)} %bitcast.196, bf16[4608,3072]{1,0:T(8,128)(2,1)} %bitcast.179), kind=kOutput, calls=%fused_computation.96 | convolution fusion | flops 7247757312 | bytes 33816576 | tf_op jit(solution)/shard_map/dot_general | solution.py:8
  127.7 3.5 fusion.8
  143.2 15.1 %all-gather.5 = bf16[1536,256]{1,0:T(8,128)(2,1)} all-gather(bf16[384,256]{1,0:T(8,128)(2,1)S(1)} %copy-done.16), channel_id=7, replica_groups=mesh['dp'=4,'hidden'=8] {'dp'}, dimensions={0}, use_global_device_ids=true | all-gather | bytes 983040 | tf_op jit(solution)/shard_map/all_gather | solution.py:44
  158.3 2.1 convolution_bitcast_fusion.6
  161.1 16.0 %convolution_bitcast_fusion.1 = f32[4608,256]{0,1:T(8,128)} fusion(bf16[256,3072]{1,0:T(8,128)(2,1)S(1)} %copy-done.5, bf16[4608,3072]{1,0:T(8,128)(2,1)} %bitcast.180), kind=kOutput, calls=%fused_computation.5 | convolution fusion | flops 7247757312 | bytes 34603008 | tf_op jit(solution)/shard_map/dot_general | solution.py:8
  177.1 6.5 %reshape.69 = f32[3,2,768,256]{2,1,0,3:T(2,128)} reshape(f32[4608,256]{0,1:T(8,128)} %convolution_bitcast_fusion.1) | data formatting | bytes 9437184 | tf_op jit(solution)/shard_map/reshape | solution.py:128
  183.6 31.2 %all-reduce.3 = bf16[384,256]{1,0:T(8,128)(2,1)S(1)} all-reduce(f32[384,256]{1,0:T(8,128)S(1)} %pad_maximum_fusion.6), channel_id=1, replica_groups=mesh['dp'=4,'hidden'=8] {'hidden'}, use_global_device_ids=true, to_apply=%region_1.2 | all-reduce | flops 98304 | bytes 589824 | tf_op jit(solution)/shard_map/psum | solution.py:119
  214.8 14.9 %convolution_bitcast_fusion = f32[4608,256]{0,1:T(8,128)} fusion(bf16[256,3072]{1,0:T(8,128)(2,1)S(1)} %copy-done.6, bf16[4608,3072]{1,0:T(8,128)(2,1)} %bitcast.182), kind=kOutput, calls=%fused_computation.4 | convolution fusion | flops 7247757312 | bytes 34603008 | tf_op jit(solution)/shard_map/dot_general | solution.py:8
  229.7 8.3 %copy.54 = bf16[4,3,768,256]{3,0,2,1:T(4,128)(2,1)} copy(bf16[4,3,768,256]{3,2,1,0:T(8,128)(2,1)} %bitcast.187) | data formatting | bytes 9437184 | tf_op jit(solution)/shard_map/all_gather | solution.py:44
  238.0 2.1 constant_dynamic-slice_fusion.2
  241.8 6.6 %reshape.71 = f32[3,2,768,256]{2,1,0,3:T(2,128)} reshape(f32[4608,256]{0,1:T(8,128)} %convolution_bitcast_fusion) | data formatting | bytes 9437184 | tf_op jit(solution)/shard_map/reshape | solution.py:129
  248.5 4.6 constant_dynamic-slice_fusion
  255.9 2.0 constant_dynamic-slice_fusion.3
  257.9 2.0 constant_dynamic-slice_fusion.1
  260.0 1.5 bitcast_add_fusion.1
  261.5 1.4 copy-done.3
  265.0 8.2 %copy.50 = bf16[4,3,768,256]{3,0,2,1:T(4,128)(2,1)} copy(bf16[4,3,768,256]{3,2,1,0:T(8,128)(2,1)} %bitcast.192) | data formatting | bytes 9437184 | tf_op jit(solution)/shard_map/all_gather | solution.py:44
  273.1 1.6 bitcast_add_fusion
  274.7 1.4 copy-done.4
  276.2 1.7 collective-permute-start.10
  277.9 4.1 collective-permute-done.4
  283.0 18.0 %all-gather.4 = bf16[1536,256]{1,0:T(8,128)(2,1)S(1)} all-gather(bf16[384,256]{1,0:T(8,128)(2,1)S(1)} %all-reduce.3), channel_id=6, replica_groups=mesh['dp'=4,'hidden'=8] {'dp'}, dimensions={0}, use_global_device_ids=true | all-gather | bytes 983040 | tf_op jit(solution)/shard_map/all_gather | solution.py:44
  301.0 1.6 fusion.34
  305.7 2.9 fusion.24
  308.6 2.9 fusion.18
  311.5 5.6 %fusion.1 = f32[3072,192]{0,1:T(8,128)} fusion(bf16[4,256,3072]{2,1,0:T(8,128)(2,1)} %bitcast.201, bf16[384,4,256]{2,0,1:T(8,128)(2,1)S(1)} %bitcast.203), kind=kOutput, calls=%fused_computation.17 | convolution fusion | flops 1208549376 | bytes 9043968 | tf_op jit(solution)/shard_map/dot_general | solution.py:8
  317.1 5.7 %fusion = f32[192,3072]{1,0:T(8,128)} fusion(bf16[4,256,3072]{2,1,0:T(8,128)(2,1)} %bitcast.202, bf16[384,4,256]{2,0,1:T(8,128)(2,1)S(1)} %bitcast.204), kind=kOutput, calls=%fused_computation.16 | convolution fusion | flops 1208549376 | bytes 9043968 | tf_op jit(solution)/shard_map/dot_general | solution.py:8
  322.9 11.7 %select_bitcast_fusion.1 = (bf16[4,3,1,768,256]{4,0,3,2,1:T(4,128)(2,1)S(1)}, bf16[4,3,1,768,256]{4,0,3,2,1:T(4,128)(2,1)S(1)}) fusion(bf16[4,3,768,256]{3,0,2,1:T(4,128)(2,1)} %collective-permute-done.13, pred[]{:T(512)S(6)} %eq.41, bf16[4,3,768,256]{3,2,1,0:T(8,128)(2,1)S(1)} %bitcast.191), kind=kLoop, calls=%fused_computation.7 | loop fusion | flops 4718592 | bytes 18874368 | tf_op jit(solution)/shard_map/stack | solution.py:36
  334.6 8.0 %pad_maximum_fusion = bf16[4,3,2,768,256]{4,0,3,2,1:T(4,128)(2,1)} fusion(bf16[4,3,1,768,256]{4,0,3,2,1:T(4,128)(2,1)S(1)} %get-tuple-element.33, bf16[4,3,1,768,256]{4,0,3,2,1:T(4,128)(2,1)S(1)} %get-tuple-element.32), kind=kLoop, calls=%fused_computation.3 | loop fusion | flops 4718592 | bytes 18874368 | tf_op jit(solution)/shard_map/stack | solution.py:36
  342.6 10.4 %copy.66 = bf16[576,8,4,256]{3,1,2,0:T(8,128)(2,1)} copy(bf16[576,8,4,256]{3,2,1,0:T(4,128)(2,1)} %bitcast.177) | data formatting | bytes 18874368
  353.0 11.2 %select_bitcast_fusion.3 = (bf16[4,3,1,768,256]{4,0,3,1,2:T(4,128)(2,1)S(1)}, bf16[4,3,1,768,256]{4,0,3,1,2:T(4,128)(2,1)S(1)}) fusion(bf16[4,3,768,256]{3,0,2,1:T(4,128)(2,1)} %collective-permute-done.12, pred[]{:T(512)S(6)} %eq.41, bf16[4,3,768,256]{3,2,1,0:T(8,128)(2,1)} %bitcast.194), kind=kLoop, calls=%fused_computation.9 | loop fusion | flops 4718592 | bytes 18874368 | tf_op jit(solution)/shard_map/stack | solution.py:36
  364.3 7.2 %maximum_bitcast_fusion = bf16[3,2,768,4,256]{4,3,2,0,1:T(4,128)(2,1)S(1)} fusion(bf16[4,3,1,768,256]{4,0,3,1,2:T(4,128)(2,1)S(1)} %get-tuple-element.35, bf16[4,3,1,768,256]{4,0,3,1,2:T(4,128)(2,1)S(1)} %get-tuple-element.34), kind=kLoop, calls=%fused_computation.2 | loop fusion | flops 4718592 | bytes 18874368 | tf_op jit(solution)/shard_map/transpose | solution.py:50
  371.5 4.6 copy.52
  376.1 10.5 %copy.65 = bf16[576,8,4,256]{3,1,2,0:T(8,128)(2,1)} copy(bf16[576,8,4,256]{3,2,1,0:T(4,128)(2,1)} %bitcast.178) | data formatting | bytes 18874368
  386.6 37.5 %convolution_multiply_fusion.1 = f32[4608,3072]{1,0:T(8,128)} fusion(bf16[4608,1024]{1,0:T(8,128)(2,1)} %bitcast.200, bf16[1024,3072]{1,0:T(8,128)(2,1)} %all-gather.13.cloned.1.call-done), kind=kOutput, calls=%fused_computation.1 | convolution fusion | flops 29005185024 | bytes 72351744 | tf_op jit(solution)/shard_map/dot_general | solution.py:8
  424.1 35.6 %convolution_multiply_fusion = f32[4608,3072]{1,0:T(8,128)} fusion(bf16[4608,1024]{1,0:T(8,128)(2,1)S(1)} %bitcast.199, bf16[1024,3072]{1,0:T(8,128)(2,1)} %all-gather.17.cloned.1.call-done), kind=kOutput, calls=%fused_computation | convolution fusion | flops 29005185024 | bytes 72351744 | tf_op jit(solution)/shard_map/dot_general | solution.py:8
  (111 shorter events, 21.9 us)
Async XLA Ops:
  7.2 99.4 %copy-start = (bf16[192,3072]{1,0:T(8,128)(2,1)S(1)}, bf16[192,3072]{1,0:T(8,128)(2,1)}, u32[]{:S(2)}) copy-start(bf16[192,3072]{1,0:T(8,128)(2,1)} %param.14) | copy-start | bytes 3538948
  7.2 25.6 %copy-start.10 = (bf16[768,256]{1,0:T(8,128)(2,1)S(1)}, bf16[768,256]{1,0:T(8,128)(2,1)}, u32[]{:S(2)}) copy-start(bf16[768,256]{1,0:T(8,128)(2,1)} %param.9) | copy-start | bytes 1179652
  7.2 222.5 %all-gather.15.cloned.1.call-start = ((), (), s32[]{:S(2)}) async-start(), calls=%async_computation.2 | async-start | bytes 5898240 | tf_op jit(solution)/shard_map/all_gather | solution.py:44
  7.2 20.7 %collective-permute-start.6 = (bf16[768,256]{1,0:T(8,128)(2,1)}, bf16[768,256]{1,0:T(8,128)(2,1)S(1)}, u32[]{:S(2)}, u32[]{:S(2)}) collective-permute-start(bf16[768,256]{1,0:T(8,128)(2,1)} %param.10), channel_id=1, source_target_pairs={{0,2},{1,3},{2,0},{3,1},{4,6},{5,7},{6,4},{7,5},{8,10},{9,11},{10,... | collective-permute-start | bytes 1179656 | tf_op jit(solution)/shard_map/ppermute | solution.py:14
  10.3 20.2 %collective-permute-start.7 = (bf16[768,256]{1,0:T(8,128)(2,1)}, bf16[768,256]{1,0:T(8,128)(2,1)S(1)}, u32[]{:S(2)}, u32[]{:S(2)}) collective-permute-start(bf16[768,256]{1,0:T(8,128)(2,1)} %param.10), channel_id=1, source_target_pairs={{0,4},{1,5},{2,6},{3,7},{4,0},{5,1},{6,2},{7,3},{8,12},{9,13},{10,... | collective-permute-start | bytes 1179656 | tf_op jit(solution)/shard_map/ppermute | solution.py:14
  32.8 232.2 %all-gather.11.cloned.1.call-start = ((), (), s32[]{:S(2)}) async-start(), calls=%async_computation | async-start | bytes 5898240 | tf_op jit(solution)/shard_map/all_gather | solution.py:44
  32.8 17.1 %collective-permute-start.1 = (bf16[768,256]{1,0:T(8,128)(2,1)S(1)}, bf16[768,256]{1,0:T(8,128)(2,1)S(1)}, u32[]{:S(2)}, u32[]{:S(2)}) collective-permute-start(bf16[768,256]{1,0:T(8,128)(2,1)S(1)} %copy-done.10), channel_id=1, source_target_pairs={{0,4},{1,5},{2,6},{3,7},{4,0},{5,1},{6,2},{7,3},{8,12},{9,13},{10,... | collective-permute-start | bytes 1179656 | tf_op jit(solution)/shard_map/ppermute | solution.py:14
  33.2 17.5 %collective-permute-start = (bf16[768,256]{1,0:T(8,128)(2,1)S(1)}, bf16[768,256]{1,0:T(8,128)(2,1)}, u32[]{:S(2)}, u32[]{:S(2)}) collective-permute-start(bf16[768,256]{1,0:T(8,128)(2,1)S(1)} %copy-done.10), channel_id=1, source_target_pairs={{0,2},{1,3},{2,0},{3,1},{4,6},{5,7},{6,4},{7,5},{8,10},{9,11},{10,... | collective-permute-start | bytes 1179656 | tf_op jit(solution)/shard_map/ppermute | solution.py:14
  50.0 0.7 copy-start.17
  53.2 258.3 %all-gather.17.cloned.1.call-start = ((), (), s32[]{:S(2)}) async-start(), calls=%async_computation.3 | async-start | bytes 7864320 | tf_op jit(solution)/shard_map/all_gather | solution.py:44
  53.3 38.0 %collective-permute-start.2 = (bf16[3,768,256]{2,1,0:T(8,128)(2,1)}, bf16[3,768,256]{2,1,0:T(8,128)(2,1)}, u32[]{:S(2)}, u32[]{:S(2)}) collective-permute-start(bf16[3,768,256]{2,1,0:T(8,128)(2,1)} %pad_maximum_fusion.3), channel_id=1, source_target_pairs={{0,1},{1,0},{2,3},{3,2},{4,5},{5,4},{6,7},{7,6},{8,9},{9,8},{10,11... | collective-permute-start | bytes 3538952 | tf_op jit(solution)/shard_map/ppermute | solution.py:14
  93.0 13.6 %copy-start.15 = (bf16[384,256]{1,0:T(8,128)(2,1)S(1)}, bf16[384,256]{1,0:T(8,128)(2,1)}, u32[]{:S(2)}) copy-start(bf16[384,256]{1,0:T(8,128)(2,1)} %all-reduce.2) | copy-start | bytes 589828
  106.6 3.7 copy-start.7
  110.2 206.9 %all-gather.13.cloned.1.call-start = ((), (), s32[]{:S(2)}) async-start(), calls=%async_computation.1 | async-start | bytes 7864320 | tf_op jit(solution)/shard_map/all_gather | solution.py:44
  110.2 2.9 collective-permute-start.8
  113.7 13.9 %copy-start.13 = (bf16[3072,192]{0,1:T(8,128)(2,1)S(1)}, bf16[3072,192]{0,1:T(8,128)(2,1)}, u32[]{:S(2)}) copy-start(bf16[3072,192]{0,1:T(8,128)(2,1)} %param.15) | copy-start | bytes 3538948
  113.8 13.9 %copy-start.16 = (bf16[384,256]{1,0:T(8,128)(2,1)S(1)}, bf16[384,256]{1,0:T(8,128)(2,1)}, u32[]{:S(2)}) copy-start(bf16[384,256]{1,0:T(8,128)(2,1)} %all-reduce.2) | copy-start | bytes 589828
  113.8 13.9 %copy-start.18 = (f32[256,3072]{1,0:T(8,128)S(1)}, f32[256,3072]{1,0:T(8,128)}, u32[]{:S(2)}) copy-start(f32[256,3072]{1,0:T(8,128)} %get-tuple-element.57) | copy-start | bytes 9437188
  131.2 29.2 %copy-start.5 = (bf16[256,3072]{1,0:T(8,128)(2,1)S(1)}, bf16[256,3072]{1,0:T(8,128)(2,1)}, u32[]{:S(2)}) copy-start(bf16[256,3072]{1,0:T(8,128)(2,1)} %get-tuple-element.56) | copy-start | bytes 4718596
  143.2 17.2 %copy-start.14 = (bf16[3072,192]{0,1:T(8,128)(2,1)S(1)}, bf16[3072,192]{0,1:T(8,128)(2,1)}, u32[]{:S(2)}) copy-start(bf16[3072,192]{0,1:T(8,128)(2,1)} %param.15) | copy-start | bytes 3538948
  177.1 37.7 %copy-start.6 = (bf16[256,3072]{1,0:T(8,128)(2,1)S(1)}, bf16[256,3072]{1,0:T(8,128)(2,1)}, u32[]{:S(2)}) copy-start(bf16[256,3072]{1,0:T(8,128)(2,1)} %fusion.8) | copy-start | bytes 4718596
  229.7 8.3 %copy-start.2 = (f32[3,2,768,256]{2,1,0,3:T(2,128)S(1)}, f32[3,2,768,256]{2,1,0,3:T(2,128)}, u32[]{:S(2)}) copy-start(f32[3,2,768,256]{2,1,0,3:T(2,128)} %reshape.69) | copy-start | bytes 14155780
  238.0 84.9 %collective-permute-start.13 = (bf16[4,3,768,256]{3,0,2,1:T(4,128)(2,1)}, bf16[4,3,768,256]{3,0,2,1:T(4,128)(2,1)}, u32[]{:S(2)}, u32[]{:S(2)}) collective-permute-start(bf16[4,3,768,256]{3,0,2,1:T(4,128)(2,1)} %copy.54), channel_id=1, source_target_pairs={{0,1},{1,0},{2,3},{3,2},{4,5},{5,4},{6,7},{7,6},{8,9},{9,8},{10,11... | collective-permute-start | bytes 14155784 | tf_op jit(solution)/shard_map/ppermute | solution.py:14
  241.3 18.7 %collective-permute-start.3 = (bf16[3,768,256]{1,2,0:T(8,128)(2,1)}, bf16[3,768,256]{1,2,0:T(8,128)(2,1)}, u32[]{:S(2)}, u32[]{:S(2)}) collective-permute-start(bf16[3,768,256]{1,2,0:T(8,128)(2,1)} %bitcast.175), channel_id=1, source_target_pairs={{0,1},{1,0},{2,3},{3,2},{4,5},{5,4},{6,7},{7,6},{8,9},{9,8},{10,11... | collective-permute-start | bytes 3538952 | tf_op jit(solution)/shard_map/ppermute | solution.py:14
  241.8 12.5 %copy-start.11 = (bf16[768,192]{0,1:T(8,128)(2,1)S(1)}, bf16[768,192]{0,1:T(8,128)(2,1)}, u32[]{:S(2)}) copy-start(bf16[768,192]{0,1:T(8,128)(2,1)} %param.13) | copy-start | bytes 884740
  241.8 14.0 %slice-start = ((s8[4718592]{0:T(1024)(128)(4,1)}), s8[524288]{0:T(1024)(128)(4,1)S(1)}, s32[]{:S(2)}) async-start(s8[4718592]{0:T(1024)(128)(4,1)} %bitcast.183), calls=%async_computation.4 | async-start | bytes 1048576
  248.4 7.4 %slice-start.1 = ((s8[4718592]{0:T(1024)(128)(4,1)}), s8[4194304]{0:T(1024)(128)(4,1)S(1)}, s32[]{:S(2)}) async-start(s8[4718592]{0:T(1024)(128)(4,1)} %bitcast.183), calls=%async_computation.5 | async-start | bytes 8388608
  248.5 9.4 %slice-start.2 = ((s8[4718592]{0:T(1024)(128)(4,1)}), s8[4194304]{0:T(1024)(128)(4,1)S(1)}, s32[]{:S(2)}) async-start(s8[4718592]{0:T(1024)(128)(4,1)} %bitcast.185), calls=%async_computation.6 | async-start | bytes 8388608
  253.1 1.5 copy-start.12
  253.1 4.8 %slice-start.3 = ((s8[4718592]{0:T(1024)(128)(4,1)}), s8[524288]{0:T(1024)(128)(4,1)S(1)}, s32[]{:S(2)}) async-start(s8[4718592]{0:T(1024)(128)(4,1)} %bitcast.185), calls=%async_computation.7 | async-start | bytes 1048576
  254.3 18.8 %collective-permute-start.9 = (bf16[3,768,256]{1,2,0:T(8,128)(2,1)}, bf16[3,768,256]{1,2,0:T(8,128)(2,1)}, u32[]{:S(2)}, u32[]{:S(2)}) collective-permute-start(bf16[3,768,256]{1,2,0:T(8,128)(2,1)} %bitcast.176), channel_id=1, source_target_pairs={{0,1},{1,0},{2,3},{3,2},{4,5},{5,4},{6,7},{7,6},{8,9},{9,8},{10,11... | collective-permute-start | bytes 3538952 | tf_op jit(solution)/shard_map/ppermute | solution.py:14
  261.5 1.4 copy-start.3
  263.9 18.2 %collective-permute-start.4 = (bf16[768,256]{0,1:T(8,128)(2,1)}, bf16[768,256]{0,1:T(8,128)(2,1)}, u32[]{:S(2)}, u32[]{:S(2)}) collective-permute-start(bf16[768,256]{0,1:T(8,128)(2,1)} %get-tuple-element.38), channel_id=1, source_target_pairs={{0,2},{1,3},{2,0},{3,1},{4,6},{5,7},{6,4},{7,5},{8,10},{9,11},{10,... | collective-permute-start | bytes 1179656 | tf_op jit(solution)/shard_map/ppermute | solution.py:14
  263.9 37.2 %collective-permute-start.5 = (bf16[768,256]{0,1:T(8,128)(2,1)}, bf16[768,256]{0,1:T(8,128)(2,1)}, u32[]{:S(2)}, u32[]{:S(2)}) collective-permute-start(bf16[768,256]{0,1:T(8,128)(2,1)} %get-tuple-element.39), channel_id=1, source_target_pairs={{0,4},{1,5},{2,6},{3,7},{4,0},{5,1},{6,2},{7,3},{8,12},{9,13},{10,... | collective-permute-start | bytes 1179656 | tf_op jit(solution)/shard_map/ppermute | solution.py:14
  273.1 27.9 %copy-start.9 = (f32[768,256]{0,1:T(8,128)S(1)}, f32[768,256]{0,1:T(8,128)}, u32[]{:S(2)}) copy-start(f32[768,256]{0,1:T(8,128)} %convolution_bitcast_fusion.5) | copy-start | bytes 2359300
  273.1 79.9 %collective-permute-start.12 = (bf16[4,3,768,256]{3,0,2,1:T(4,128)(2,1)}, bf16[4,3,768,256]{3,0,2,1:T(4,128)(2,1)}, u32[]{:S(2)}, u32[]{:S(2)}) collective-permute-start(bf16[4,3,768,256]{3,0,2,1:T(4,128)(2,1)} %copy.50), channel_id=1, source_target_pairs={{0,1},{1,0},{2,3},{3,2},{4,5},{5,4},{6,7},{7,6},{8,9},{9,8},{10,11... | collective-permute-start | bytes 14155784 | tf_op jit(solution)/shard_map/ppermute | solution.py:14
  274.7 1.4 copy-start.4
  276.2 27.3 %collective-permute-start.10 = (bf16[768,256]{0,1:T(8,128)(2,1)S(1)}, bf16[768,256]{0,1:T(8,128)(2,1)S(1)}, u32[]{:S(2)}, u32[]{:S(2)}) collective-permute-start(bf16[768,256]{0,1:T(8,128)(2,1)S(1)} %get-tuple-element.36), channel_id=1, source_target_pairs={{0,2},{1,3},{2,0},{3,1},{4,6},{5,7},{6,4},{7,5},{8,10},{9,11},{10,... | collective-permute-start | bytes 1179656 | tf_op jit(solution)/shard_map/ppermute | solution.py:14
  282.0 21.5 %collective-permute-start.11 = (bf16[768,256]{0,1:T(8,128)(2,1)S(1)}, bf16[768,256]{0,1:T(8,128)(2,1)S(1)}, u32[]{:S(2)}, u32[]{:S(2)}) collective-permute-start(bf16[768,256]{0,1:T(8,128)(2,1)S(1)} %get-tuple-element.37), channel_id=1, source_target_pairs={{0,4},{1,5},{2,6},{3,7},{4,0},{5,1},{6,2},{7,3},{8,12},{9,13},{10,... | collective-permute-start | bytes 1179656 | tf_op jit(solution)/shard_map/ppermute | solution.py:14
  304.8 6.7 %copy-start.8 = (bf16[1536,256]{1,0:T(8,128)(2,1)S(1)}, bf16[1536,256]{1,0:T(8,128)(2,1)}, u32[]{:S(2)}) copy-start(bf16[1536,256]{1,0:T(8,128)(2,1)} %all-gather.5) | copy-start | bytes 2359300
  317.1 5.7 %slice-start.4 = ((s8[4718592]{0:T(1024)(128)(4,1)}), s8[4194304]{0:T(1024)(128)(4,1)S(1)}, s32[]{:S(2)}) async-start(s8[4718592]{0:T(1024)(128)(4,1)} %bitcast.189), calls=%async_computation.8 | async-start | bytes 8388608
  317.1 5.7 %slice-start.5 = ((s8[4718592]{0:T(1024)(128)(4,1)}), s8[524288]{0:T(1024)(128)(4,1)S(1)}, s32[]{:S(2)}) async-start(s8[4718592]{0:T(1024)(128)(4,1)} %bitcast.189), calls=%async_computation.9 | async-start | bytes 1048576
  376.1 48.0 %slice-start.6 = ((s8[9437184]{0:T(1024)(128)(4,1)}), s8[1048576]{0:T(1024)(128)(4,1)S(1)}, s32[]{:S(2)}) async-start(s8[9437184]{0:T(1024)(128)(4,1)} %bitcast.197), calls=%async_computation.10 | async-start | bytes 2097152
  386.6 37.5 %slice-start.7 = ((s8[9437184]{0:T(1024)(128)(4,1)}), s8[4194304]{0:T(1024)(128)(4,1)S(1)}, s32[]{:S(2)}) async-start(s8[9437184]{0:T(1024)(128)(4,1)} %bitcast.197), calls=%async_computation.11 | async-start | bytes 8388608
  386.6 37.5 %slice-start.8 = ((s8[9437184]{0:T(1024)(128)(4,1)}), s8[4194304]{0:T(1024)(128)(4,1)S(1)}, s32[]{:S(2)}) async-start(s8[9437184]{0:T(1024)(128)(4,1)} %bitcast.197), calls=%async_computation.12 | async-start | bytes 8388608
  424.1 35.6 %copy-start.1 = (bf16[192,3072]{1,0:T(8,128)(2,1)S(1)}, bf16[192,3072]{1,0:T(8,128)(2,1)}, u32[]{:S(2)}) copy-start(bf16[192,3072]{1,0:T(8,128)(2,1)} %param.14) | copy-start | bytes 3538948
Sparse Core Ops, SparseCore 0:
  32.9 57.1 all-gather.14
  92.5 57.2 all-gather.10
  151.7 74.9 all-gather.16
  228.3 76.4 all-gather.12
